TPU v7x, 32 devices: a whole 2x2x4 slice. The times are simulated.
32 devices in a mesh: row: 8 (over y, x, core), col: 4 (over z).
Axes of the slice: x: 2, y: 2, z: 4, core: 2. Of those that a mesh axis runs over, the one named last changes fastest.
Arguments:
- train_grads: bfloat16 [4096, 8192], P('row', 'col'), may hold values from -16 to 16
- query_grads: bfloat16 [2048, 8192], P('col', 'row'), may hold values from -6 to 6
Outputs:
- scores: float32 [4096, 2048], P('row', 'col')
All inputs are finite; a program needn't handle non-finite values.
Results may differ from a plain program's by a relative error of at most 0.0081.
Values may be sent and summed in bfloat16 or wider, within the bound.
A program may use at most 128 MiB of HBM per device.

v0:
```python
import functools
import math

import jax
import jax.numpy as jnp
from jax import lax
from jax.experimental import pallas as pl
from jax.experimental.pallas import tpu as pltpu
from jax.sharding import PartitionSpec as P

PROJ = 64
LAYERS = 2
MESH = pl.DeviceIdType.MESH

damping_ratio = 0.1


def factor_terms(block):
    input_side = jnp.einsum("noi,noj->ij", block, block, preferred_element_type=jnp.float32)
    output_side = jnp.einsum("noi,npi->op", block, block, preferred_element_type=jnp.float32)
    return input_side, output_side


def sum_kernel(rows, group, x_ref, out_ref, buf, send_sem, recv_sem):
    row, col = lax.axis_index("row"), lax.axis_index("col")
    first = lax.div(col, group) * group
    index = row * group + lax.rem(col, group)
    count = rows * group

    def peer(step):
        other = lax.rem(index + step, count)
        return lax.div(other, group), first + lax.rem(other, group)

    barrier = pltpu.get_barrier_semaphore()
    for step in range(1, count):
        pl.semaphore_signal(barrier, inc=1, device_id=peer(step), device_id_type=MESH)
    pl.semaphore_wait(barrier, count - 1)
    copies = []
    for step in range(1, count):
        copy = pltpu.make_async_remote_copy(
            src_ref=x_ref,
            dst_ref=buf.at[step - 1],
            send_sem=send_sem.at[step - 1],
            recv_sem=recv_sem.at[step - 1],
            device_id=peer(step),
            device_id_type=MESH,
        )
        copy.start()
        copies.append(copy)
    total = x_ref[...]
    for step in range(1, count):
        copies[step - 1].wait_recv()
        total = total + buf[step - 1]
    out_ref[...] = total
    for copy in copies:
        copy.wait_send()


def sum_over_group(terms, rows, group):
    count = rows * group
    return pl.pallas_call(
        functools.partial(sum_kernel, rows, group),
        out_shape=jax.ShapeDtypeStruct(terms.shape, jnp.float32),
        in_specs=[pl.BlockSpec(memory_space=pltpu.VMEM)],
        out_specs=pl.BlockSpec(memory_space=pltpu.VMEM),
        scratch_shapes=[
            pltpu.VMEM((count - 1,) + terms.shape, jnp.float32),
            pltpu.SemaphoreType.DMA((count - 1,)),
            pltpu.SemaphoreType.DMA((count - 1,)),
        ],
        compiler_params=pltpu.CompilerParams(collective_id=0, has_side_effects=True),
    )(terms)


def invert_kernel(scale, x_ref, out_ref):
    size = PROJ
    across = lax.broadcasted_iota(jnp.int32, (size, size), 1)
    down = lax.broadcasted_iota(jnp.int32, (size, size), 0)
    diagonal = across == down
    states = []
    for side in range(2):
        factor = x_ref[side] * scale
        trace = jnp.sum(jnp.sum(jnp.where(diagonal, factor, 0.0), axis=1, keepdims=True), axis=0, keepdims=True)
        states.append(factor + jnp.where(diagonal, damping_ratio * (trace / size), 0.0))
    for k in range(size):
        for side in range(2):
            value = states[side]
            column = value[:, k : k + 1]
            row = value[k : k + 1, :]
            inverse_pivot = 1.0 / value[k : k + 1, k : k + 1]
            unit_row = jnp.where(across[:1] == k, 1.0, row) * inverse_pivot
            cleared = jnp.where(across == k, 0.0, value)
            updated = cleared - column * unit_row
            states[side] = jnp.where(down == k, unit_row, updated)
    for side in range(2):
        out_ref[side] = states[side].astype(jnp.bfloat16)


def invert(factors, scale):
    return pl.pallas_call(
        functools.partial(invert_kernel, scale),
        out_shape=jax.ShapeDtypeStruct((2, PROJ, PROJ), jnp.bfloat16),
        in_specs=[pl.BlockSpec(memory_space=pltpu.VMEM)],
        out_specs=pl.BlockSpec(memory_space=pltpu.VMEM),
    )(factors)


def picks(parts, order, axis):
    return jnp.concatenate(
        [lax.dynamic_index_in_dim(parts, index, axis, keepdims=False) for index in order], axis=axis
    )


def local(rows, cols, train_grads, query_grads):
    group = cols // LAYERS
    row, col = lax.axis_index("row"), lax.axis_index("col")
    place = lax.rem(col, group)
    layer = lax.div(col, group)
    count, width = train_grads.shape
    part = count // group
    outputs = width // PROJ

    def shifted(value, step):
        pairs = [(c, c // group * group + (c + step) % group) for c in range(cols)]
        return lax.ppermute(value, "col", pairs)

    def chunk(index):
        return lax.dynamic_slice_in_dim(train_grads, lax.rem(index, group) * part, part, 0)

    turns = []
    for k in range(group):
        pieces = [chunk(place + k)]
        for step in range(1, group):
            pieces.append(shifted(chunk(place + step + k), step))
        turns.append(jnp.stack(pieces, axis=1))

    def to_order(value, axis):
        parts = value.reshape(value.shape[:axis] + (group, value.shape[axis] // group) + value.shape[axis + 1 :])
        return picks(parts, [lax.rem(place - t + group, group) for t in range(group)], axis)

    input_side, output_side = factor_terms(turns[0].reshape(part, PROJ, PROJ))
    output_side = to_order(to_order(output_side, 0), 1)
    factors = sum_over_group(jnp.stack([input_side, output_side]), rows, group)
    inverses = invert(factors, 1.0 / (count * rows * PROJ))

    half_rows = rows // LAYERS
    swaps = []
    for r in range(rows):
        for c in range(cols):
            if r // half_rows != c // group:
                source = r * cols + c
                swaps.append((source, (r + half_rows) % rows * cols + (c + group) % cols))
            else:
                swaps.append((r * cols + c, r * cols + c))
    own_query = lax.ppermute(query_grads, ("row", "col"), swaps)
    queries = lax.all_gather(own_query, "row", axis=0)
    query_count, query_width = query_grads.shape
    queries = queries.reshape(LAYERS, half_rows, query_count, query_width)

    examples = jnp.concatenate(turns, axis=0).reshape(count, PROJ, PROJ)
    half = jnp.einsum(
        "noi,ij->noj", examples, inverses[0], preferred_element_type=jnp.float32
    ).astype(jnp.bfloat16)
    conditioned = jnp.einsum(
        "op,npj->noj", to_order(inverses[1], 1), half, preferred_element_type=jnp.float32
    ).astype(jnp.bfloat16)
    conditioned = conditioned.reshape(count, half_rows, query_width)
    product = jnp.einsum(
        "nqf,sqmf->snm", conditioned, queries, preferred_element_type=jnp.float32
    ) * (1.0 / math.sqrt(LAYERS * PROJ * PROJ))
    kept = jnp.where(layer == 0, product[0], product[1])
    given = jnp.where(layer == 0, product[1], product[0]).astype(jnp.bfloat16)
    pairs = [(c, (c + group) % cols) for c in range(cols)]
    result = kept + lax.ppermute(given, "col", pairs).astype(jnp.float32)
    pieces = result.reshape(group, part, query_count)
    return picks(pieces, [lax.rem(t - place + group, group) for t in range(group)], 0)


def solution(mesh):
    placed = (P("row", "col"), P("col", "row"))
    rows, cols = mesh.shape["row"], mesh.shape["col"]
    return jax.shard_map(
        functools.partial(local, rows, cols),
        mesh=mesh,
        in_specs=placed,
        out_specs=P("row", "col"),
        check_vma=False,
    )
```

profile of v0, /device:TPU:0, one launch (start us, length us, event | category | flops | bytes accessed | tf_op | source)
XLA Modules:
  0.0 187.6 jit_solution(15508493843735329265)
XLA Ops:
  6.5 0.0 all-gather.3.cloned.1.call-start
  6.5 1.9 collective-permute-start.2
  8.4 0.0 collective-permute-done.2
  8.4 0.0 copy-start.1
  8.4 1.0 copy-done.1
  9.5 0.0 all-gather.3.cloned.1.call-update
  9.5 2.2 %constant_dynamic-slice_fusion.6 = (bf16[256,2048]{1,0:T(8,128)(2,1)S(1)}, bf16[256,2048]{1,0:T(8,128)(2,1)S(1)}, bf16[256,2048]{1,0:T(8,128)(2,1)S(1)}) fusion(bf16[512,2048]{1,0:T(8,128)(2,1)} %param.2, s32[]{:T(128)S(6)} %select_n.47, s32[]{:T(128)S(6)} %select_n.48, s32[]{:T(128)S(6)} %select_n.49), kind=kLoop, calls=%fused_computation.36 | loop fusion | bytes 6291468 | tf_op jit(solution)/shard_map/dynamic_slice | solution.py:128
  11.7 1.3 copy.21
  13.0 3.0 %collective-permute-start = (bf16[256,2048]{0,1:T(8,128)(2,1)}, bf16[256,2048]{0,1:T(8,128)(2,1)S(1)}, u32[]{:S(2)}, u32[]{:S(2)}) collective-permute-start(bf16[256,2048]{0,1:T(8,128)(2,1)} %copy.21), channel_id=1, source_target_pairs={{0,1},{1,0},{2,3},{3,2},{4,5},{5,4},{6,7},{7,6},{8,9},{9,8},{10,11... | collective-permute-start | bytes 3145736 | tf_op jit(solution)/shard_map/ppermute | solution.py:125
  16.0 1.3 copy.22
  17.3 0.0 collective-permute-start.1
  17.3 0.5 copy.6
  17.9 43.7 %collective-permute-done = bf16[256,2048]{0,1:T(8,128)(2,1)S(1)} collective-permute-done((bf16[256,2048]{0,1:T(8,128)(2,1)}, bf16[256,2048]{0,1:T(8,128)(2,1)S(1)}, u32[]{:S(2)}, u32[]{:S(2)}) %collective-permute-start) | collective-permute-done | bytes 1048608 | tf_op jit(solution)/shard_map/ppermute | solution.py:125
  61.6 0.0 copy-start
  61.6 1.0 copy-done
  62.6 1.4 pad_maximum_fusion
  64.0 4.4 %fusion.6 = f32[2,32,64]{2,1,0:T(8,128)S(1)} fusion(bf16[256,64,64]{0,2,1:T(8,128)(2,1)S(1)} %bitcast.64, bf16[2,32,64,256]{3,2,1,0:T(8,128)(2,1)S(1)} %bitcast.65), kind=kOutput, calls=%fused_computation.11 | convolution fusion | flops 134217728 | bytes 4210688 | tf_op jit(solution)/shard_map/noi,npi->op/dot_general | solution.py:20
  68.4 0.1 concatenate.21
  68.5 0.1 concatenate.22
  68.6 0.1 constant_dynamic-slice_fusion.1
  68.7 0.1 maximum_bitcast_fusion
  68.8 0.7 convolution_bitcast_fusion
  69.5 0.6 pad_maximum_fusion.2.x_ref
  70.1 50.6 %shard_map.28.x_ref = f32[2,64,64]{2,1,0:T(8,128)} custom-call(f32[2,64,64]{2,1,0:T(8,128)} %pad_maximum_fusion.2.x_ref), custom_call_target="tpu_custom_call" | custom-call | tf_op jit(solution)/shard_map/pallas_call | solution.py:61
  120.7 7.0 %shard_map.29 = bf16[2,64,64]{2,1,0:T(8,128)(2,1)} custom-call(f32[2,64,64]{2,1,0:T(8,128)} %shard_map.28.x_ref), custom_call_target="tpu_custom_call" | custom-call | tf_op jit(solution)/shard_map/pallas_call | solution.py:100
  127.8 0.7 slice.18
  128.5 0.1 copy.11
  128.6 0.1 copy.12
  128.7 0.1 copy.13
  128.8 0.0 collective-permute-done.1
  128.8 0.0 copy-start.2
  128.8 2.2 %maximum_maximum_fusion = bf16[512,2,2048]{0,2,1:T(8,128)(2,1)S(1)} fusion(bf16[256,1,2048]{0,2,1:T(8,128)(2,1)} %bitcast.3, bf16[256,1,2048]{0,2,1:T(8,128)(2,1)} %bitcast.72, bf16[256,1,2048]{0,2,1:T(8,128)(2,1)} %bitcast.74, bf16[256,1,2048]{0,2,1:T(8,128)(2,1)S(1)} %bitcast.69), kind=kLoop, calls=%fused_computation.2 | loop fusion | flops 16777216 | bytes 8388608 | tf_op jit(solution)/shard_map/concatenate | solution.py:160
  131.0 0.0 copy-done.2
  131.0 1.3 fusion.12
  132.3 5.5 %convert_bitcast_fusion = bf16[512,64,64]{0,1,2:T(8,128)(2,1)S(1)} fusion(bf16[512,64,64]{0,2,1:T(8,128)(2,1)S(1)} %fusion.12, bf16[64,32]{1,0:T(8,128)(2,1)S(1)} %copy.13, bf16[64,32]{1,0:T(8,128)(2,1)S(1)} %copy.12), kind=kOutput, calls=%fused_computation.3 | convolution fusion | flops 270548992 | bytes 8396800 | tf_op jit(solution)/shard_map/op,npj->noj/dot_general | solution.py:164
  137.8 4.3 %copy.14 = bf16[512,64,64]{0,2,1:T(8,128)(2,1)} copy(bf16[512,64,64]{0,1,2:T(8,128)(2,1)S(1)} %convert_bitcast_fusion) | data formatting | bytes 8388608 | tf_op jit(solution)/shard_map/convert_element_type | solution.py:166
  142.1 0.0 all-gather.3.cloned.1.call-done
  142.1 8.3 %fusion.1 = f32[2,512,512]{2,1,0:T(8,128)S(1)} fusion(bf16[512,4,1024,1]{0,2,1,3:T(8,128)(2,1)} %bitcast.70, bf16[2,4,512,1024]{3,2,1,0:T(8,128)(2,1)} %bitcast.78), kind=kOutput, calls=%fused_computation.6 | convolution fusion | flops 4295491584 | bytes 14680064 | tf_op jit(solution)/shard_map/nqf,sqmf->snm/dot_general | solution.py:168
  150.4 0.1 fusion.11
  150.5 5.4 %collective-permute-start.3 = (bf16[512,512]{1,0:T(8,128)(2,1)S(1)}, bf16[512,512]{1,0:T(8,128)(2,1)S(1)}, u32[]{:S(2)}, u32[]{:S(2)}) collective-permute-start(bf16[512,512]{1,0:T(8,128)(2,1)S(1)} %fusion.11), channel_id=1, source_target_pairs={{0,2},{1,3},{2,0},{3,1},{4,6},{5,7},{6,4},{7,5},{8,10},{9,11},{10,... | collective-permute-start | bytes 1572872 | tf_op jit(solution)/shard_map/ppermute | solution.py:174
  156.0 23.4 %collective-permute-done.3 = bf16[512,512]{1,0:T(8,128)(2,1)S(1)} collective-permute-done((bf16[512,512]{1,0:T(8,128)(2,1)S(1)}, bf16[512,512]{1,0:T(8,128)(2,1)S(1)}, u32[]{:S(2)}, u32[]{:S(2)}) %collective-permute-start.3) | collective-permute-done | bytes 524320 | tf_op jit(solution)/shard_map/ppermute | solution.py:174
  179.4 0.3 bitcast_add_fusion
  179.7 0.1 dynamic-slice_bitcast_fusion.1
  179.8 1.0 pad_maximum_fusion.1
  (4 shorter events, 0.0 us)
Async XLA Ops:
  6.5 135.6 %all-gather.3.cloned.1.call-start = ((), (), s32[]{:S(2)}) async-start(), calls=%async_computation | async-start | bytes 9437184 | tf_op jit(solution)/shard_map/all_gather | solution.py:156
  6.5 1.9 collective-permute-start.2
  8.4 1.1 copy-start.1
  13.0 48.6 %collective-permute-start = (bf16[256,2048]{0,1:T(8,128)(2,1)}, bf16[256,2048]{0,1:T(8,128)(2,1)S(1)}, u32[]{:S(2)}, u32[]{:S(2)}) collective-permute-start(bf16[256,2048]{0,1:T(8,128)(2,1)} %copy.21), channel_id=1, source_target_pairs={{0,1},{1,0},{2,3},{3,2},{4,5},{5,4},{6,7},{7,6},{8,9},{9,8},{10,11... | collective-permute-start | bytes 3145736 | tf_op jit(solution)/shard_map/ppermute | solution.py:125
  17.3 111.5 %collective-permute-start.1 = (bf16[256,2048]{0,1:T(8,128)(2,1)}, bf16[256,2048]{0,1:T(8,128)(2,1)}, u32[]{:S(2)}, u32[]{:S(2)}) collective-permute-start(bf16[256,2048]{0,1:T(8,128)(2,1)} %copy.22), channel_id=1, source_target_pairs={{0,1},{1,0},{2,3},{3,2},{4,5},{5,4},{6,7},{7,6},{8,9},{9,8},{10,11... | collective-permute-start | bytes 3145736 | tf_op jit(solution)/shard_map/ppermute | solution.py:125
  61.6 1.0 copy-start
  128.8 2.2 %copy-start.2 = (bf16[2,64,64]{2,1,0:T(8,128)(2,1)S(1)}, bf16[2,64,64]{2,1,0:T(8,128)(2,1)}, u32[]{:S(2)}) copy-start(bf16[2,64,64]{2,1,0:T(8,128)(2,1)} %shard_map.29) | copy-start | bytes 49156
  150.5 28.9 %collective-permute-start.3 = (bf16[512,512]{1,0:T(8,128)(2,1)S(1)}, bf16[512,512]{1,0:T(8,128)(2,1)S(1)}, u32[]{:S(2)}, u32[]{:S(2)}) collective-permute-start(bf16[512,512]{1,0:T(8,128)(2,1)S(1)} %fusion.11), channel_id=1, source_target_pairs={{0,2},{1,3},{2,0},{3,1},{4,6},{5,7},{6,4},{7,5},{8,10},{9,11},{10,... | collective-permute-start | bytes 1572872 | tf_op jit(solution)/shard_map/ppermute | solution.py:174
Sparse Core Ops, SparseCore 0:
  9.6 120.3 all-gather.2
where the time goes:
time: 188 us
  waiting for transfers between devices  67.1 us (36%)
  Pallas kernels  57.6 us (31%)
  matrix products  20.2 us (11%)
  between operations  13.6 us (7%)
  local copies, waits for them, and re-layouts  13 us (7%)
  starting transfers between devices  10.3 us (5%)
  other arithmetic  5.73 us (3%)
    pallas_call x1, Pallas kernels, sum_over_group(): pl.pallas_call(functools.partial(sum_kernel, rows, group), out_shape=jax....  50.6 us
    ppermute x2, waiting for transfers between devices, shifted(): return lax.ppermute(value, 'col', pairs)  43.7 us
    ppermute x1, waiting for transfers between devices, local(): result = kept + lax.ppermute(given, 'col', pairs).astype(jnp.float32)  23.4 us
    dot_general x1, matrix products, local(): jnp.einsum('nqf,sqmf->snm', conditioned, queries, preferred_element_type=...  8.29 us
    pallas_call x1, Pallas kernels, invert(): pl.pallas_call(functools.partial(invert_kernel, scale), out_shape=jax.Sha...  7.05 us
    dot_general x1, matrix products, local(): jnp.einsum('op,npj->noj', to_order(inverses[1], 1), half, preferred_eleme...  5.49 us
    ppermute x1, starting transfers between devices, local(): result = kept + lax.ppermute(given, 'col', pairs).astype(jnp.float32)  5.44 us
    unnamed x9, local copies, waits for them, and re-layouts  4.66 us
  transfers between devices with their start and end apart: 5, of which 2 were waited for; matrix products, arithmetic and copies ran while one was open for 14% of the time, Pallas kernels for 31%

commit v1 on v0

--- a/solution.py
+++ b/solution.py
@@ -124,14 +124,23 @@
         pairs = [(c, c // group * group + (c + step) % group) for c in range(cols)]
         return lax.ppermute(value, "col", pairs)
 
+    def across(value, bit):
+        return lax.ppermute(value, "row", [(r, r ^ bit) for r in range(rows)])
+
     def chunk(index):
         return lax.dynamic_slice_in_dim(train_grads, lax.rem(index, group) * part, part, 0)
 
     turns = []
+    ready = None
     for k in range(group):
         pieces = [chunk(place + k)]
         for step in range(1, group):
-            pieces.append(shifted(chunk(place + step + k), step))
+            sent = chunk(place + step + k)
+            if ready is not None:
+                sent, _ = lax.optimization_barrier((sent, ready))
+            pieces.append(shifted(sent, step))
+        if k == 0:
+            ready = pieces[-1]
         turns.append(jnp.stack(pieces, axis=1))
 
     def to_order(value, axis):
@@ -153,26 +162,58 @@
             else:
                 swaps.append((r * cols + c, r * cols + c))
     own_query = lax.ppermute(query_grads, ("row", "col"), swaps)
-    queries = lax.all_gather(own_query, "row", axis=0)
     query_count, query_width = query_grads.shape
-    queries = queries.reshape(LAYERS, half_rows, query_count, query_width)
-
-    examples = jnp.concatenate(turns, axis=0).reshape(count, PROJ, PROJ)
-    half = jnp.einsum(
-        "noi,ij->noj", examples, inverses[0], preferred_element_type=jnp.float32
-    ).astype(jnp.bfloat16)
-    conditioned = jnp.einsum(
-        "op,npj->noj", to_order(inverses[1], 1), half, preferred_element_type=jnp.float32
-    ).astype(jnp.bfloat16)
-    conditioned = conditioned.reshape(count, half_rows, query_width)
-    product = jnp.einsum(
-        "nqf,sqmf->snm", conditioned, queries, preferred_element_type=jnp.float32
-    ) * (1.0 / math.sqrt(LAYERS * PROJ * PROJ))
-    kept = jnp.where(layer == 0, product[0], product[1])
-    given = jnp.where(layer == 0, product[1], product[0]).astype(jnp.bfloat16)
+    bits = [1 << k for k in range(1, rows.bit_length() - 1)]
+    held = []
+    for number, piece in enumerate(jnp.split(own_query, 2, axis=0)):
+        by_offset = {0: piece}
+        near_core = {}
+        for bit in (bits if number == 0 else bits[::-1]):
+            arrived = {d ^ bit: across(v, bit) for d, v in by_offset.items()}
+            by_offset.update(arrived)
+        for d, value in by_offset.items():
+            near_core[d ^ 1] = across(value, 1)
+        by_offset.update(near_core)
+        held.append(by_offset)
+
+    scale = 1.0 / math.sqrt(LAYERS * PROJ * PROJ)
+    output_inverse = to_order(inverses[1], 1)
+    own_side = lax.div(row, half_rows) == layer
+    quarter = lax.rem(row, half_rows)
     pairs = [(c, (c + group) % cols) for c in range(cols)]
-    result = kept + lax.ppermute(given, "col", pairs).astype(jnp.float32)
-    pieces = result.reshape(group, part, query_count)
+    results = []
+    for turn in turns:
+        half = jnp.einsum(
+            "noi,ij->noj", turn.reshape(part, PROJ, PROJ), inverses[0], preferred_element_type=jnp.float32
+        ).astype(jnp.bfloat16)
+        conditioned = jnp.einsum(
+            "op,npj->noj", output_inverse, half, preferred_element_type=jnp.float32
+        ).astype(jnp.bfloat16)
+        conditioned = conditioned.reshape(part, PROJ * PROJ)
+        columns = [
+            lax.dynamic_slice_in_dim(conditioned, (quarter ^ d) * query_width, query_width, 1)
+            for d in range(half_rows)
+        ]
+        sides = []
+        for side in range(LAYERS):
+            products = []
+            for by_offset in held:
+                products.append(
+                    sum(
+                        lax.dot_general(
+                            columns[d],
+                            by_offset[side * half_rows + d],
+                            (((1,), (1,)), ((), ())),
+                            preferred_element_type=jnp.float32,
+                        )
+                        for d in range(half_rows)
+                    )
+                )
+            sides.append(jnp.concatenate(products, axis=1) * scale)
+        kept = jnp.where(own_side, sides[0], sides[1])
+        given = jnp.where(own_side, sides[1], sides[0]).astype(jnp.bfloat16)
+        results.append(kept + lax.ppermute(given, "col", pairs).astype(jnp.float32))
+    pieces = jnp.stack(results)
     return picks(pieces, [lax.rem(t - place + group, group) for t in range(group)], 0)
 
 

time: 188 us -> 180 us (0.957)
  starting transfers between devices: 10.3 us -> 43.2 us
  Pallas kernels: 57.6 us -> 26.5 us
  between operations: 13.6 us -> 0.57 us
  matrix products: 20.2 us -> 31.2 us
  waiting for transfers between devices: 67.1 us -> 58.3 us
    ppermute x1 -> x16, starting transfers between devices: 5.44 us -> 37.4 us  [the longest x14 33.8 us: across(): return lax.ppermute(value, 'row', [(r, r ^ bit) for r in range(rows)])]
    pallas_call x1, Pallas kernels: 50.6 us -> 19.4 us  [sum_over_group(): pl.pallas_call(functools.partial(sum_kernel, rows, group), out_shape=jax....]
    ppermute x2, waiting for transfers between devices: 43.7 us -> 26.5 us  [shifted(): return lax.ppermute(value, 'col', pairs)]
    dot_general x3 -> x36, matrix products: 15.1 us -> 26.1 us  [the longest x32 20.5 us: local(): lax.dot_general(columns[d], by_offset[side * half_rows + d], (((1,), (1,)...]
    ppermute x1 -> x16, waiting for transfers between devices: 23.4 us -> 31.8 us  [the longest x2 22.9 us: local(): results.append(kept + lax.ppermute(given, 'col', pairs).astype(jnp.float32))]
    unnamed x9, local copies, waits for them, and re-layouts: 4.66 us -> 0.58 us
    another operation x0 -> x1, local copies, waits for them, and re-layouts: none -> 2.85 us  [local(): turns.append(jnp.stack(pieces, axis=1))]
    concatenate x1 -> x0, other arithmetic: 2.19 us -> none  [local(): examples = jnp.concatenate(turns, axis=0).reshape(count, PROJ, PROJ)]
  transfers between devices with their start and end apart: 5 -> 19, of which waited for: 2 -> 6; matrix products, arithmetic and copies ran while one was open for 14% -> 27% of each run, Pallas kernels for 31% -> 15%
where the time goes in v1:
time: 180 us; the launch traced here: 179 us
  waiting for transfers between devices  58.3 us (32%)
  starting transfers between devices  43.2 us (24%)
  matrix products  31.2 us (17%)
  Pallas kernels  26.5 us (15%)
  local copies, waits for them, and re-layouts  14.2 us (8%)
  other arithmetic  5.29 us (3%)
    ppermute x14, starting transfers between devices, across(): return lax.ppermute(value, 'row', [(r, r ^ bit) for r in range(rows)])  33.8 us
    ppermute x2, waiting for transfers between devices, shifted(): return lax.ppermute(value, 'col', pairs)  26.5 us
    ppermute x2, waiting for transfers between devices, local(): results.append(kept + lax.ppermute(given, 'col', pairs).astype(jnp.float32))  22.9 us
    dot_general x32, matrix products, local(): lax.dot_general(columns[d], by_offset[side * half_rows + d], (((1,), (1,)...  20.5 us
    pallas_call x1, Pallas kernels, sum_over_group(): pl.pallas_call(functools.partial(sum_kernel, rows, group), out_shape=jax....  19.4 us
    ppermute x14, waiting for transfers between devices, across(): return lax.ppermute(value, 'row', [(r, r ^ bit) for r in range(rows)])  8.89 us
    pallas_call x1, Pallas kernels, invert(): pl.pallas_call(functools.partial(invert_kernel, scale), out_shape=jax.Sha...  7.05 us
    dynamic_slice x2, local copies, waits for them, and re-layouts, chunk(): lax.dynamic_slice_in_dim(train_grads, lax.rem(index, group) * part, part, 0)  4.43 us
  transfers between devices with their start and end apart: 19, of which 6 were waited for; matrix products, arithmetic and copies ran while one was open for 27% of the time, Pallas kernels for 15%

profile of v1, /device:TPU:0, one launch (start us, length us, event | category | flops | bytes accessed | tf_op | source)
XLA Modules:
  0.0 179.3 jit_solution(3308116405093088822)
XLA Ops:
  0.0 1.9 %collective-permute-start.1 = (bf16[512,1024]{1,0:T(8,128)(2,1)}, bf16[512,1024]{1,0:T(8,128)(2,1)S(1)}, u32[]{:S(2)}, u32[]{:S(2)}) collective-permute-start(bf16[512,1024]{1,0:T(8,128)(2,1)} %param.3), channel_id=1, source_target_pairs={{0,0},{1,1},{2,16},{3,17},{4,4},{5,5},{6,20},{7,21},{8,8},{9,9},{1... | collective-permute-start | bytes 3145736 | tf_op jit(solution)/shard_map/ppermute | solution.py:164
  1.9 3.1 %constant_dynamic-slice_fusion = (bf16[256,2048]{1,0:T(8,128)(2,1)S(1)}, bf16[256,1,2048]{2,0,1:T(8,128)(2,1)}, bf16[256,2048]{1,0:T(8,128)(2,1)S(1)}) fusion(bf16[512,2048]{1,0:T(8,128)(2,1)} %param.2, s32[]{:T(128)S(6)} %select_n.77, s32[]{:T(128)S(6)} %select_n.67, s32[]{:T(128)S(6)} %select_n.68), kind=kLoop, calls=%fused_computation.136 | loop fusion | bytes 6291468 | tf_op jit(solution)/shard_map/dynamic_slice | solution.py:131
  5.0 3.0 %collective-permute-start = (bf16[256,2048]{1,0:T(8,128)(2,1)S(1)}, bf16[256,2048]{1,0:T(8,128)(2,1)}, u32[]{:S(2)}, u32[]{:S(2)}) collective-permute-start(bf16[256,2048]{1,0:T(8,128)(2,1)S(1)} %get-tuple-element.9), channel_id=1, source_target_pairs={{0,1},{1,0},{2,3},{3,2},{4,5},{5,4},{6,7},{7,6},{8,9},{9,8},{10,11... | collective-permute-start | bytes 3145736 | tf_op jit(solution)/shard_map/ppermute | solution.py:125
  8.0 1.3 copy.13
  9.3 1.3 copy.21
  10.6 1.1 fusion.101
  11.7 1.5 collective-permute-start.3
  13.2 0.5 collective-permute-start.5
  13.7 0.5 collective-permute-start.6
  14.2 18.4 %collective-permute-done = bf16[256,2048]{1,0:T(8,128)(2,1)} collective-permute-done((bf16[256,2048]{1,0:T(8,128)(2,1)S(1)}, bf16[256,2048]{1,0:T(8,128)(2,1)}, u32[]{:S(2)}, u32[]{:S(2)}) %collective-permute-start) | collective-permute-done | bytes 1048608 | tf_op jit(solution)/shard_map/ppermute | solution.py:125
  32.6 25.3 %collective-permute-start.8 = (bf16[256,1024]{1,0:T(8,128)(2,1)}, bf16[256,1024]{1,0:T(8,128)(2,1)}, u32[]{:S(2)}, u32[]{:S(2)}) collective-permute-start(bf16[256,1024]{1,0:T(8,128)(2,1)} %get-tuple-element.12), channel_id=1, source_target_pairs={{0,16},{4,20},{8,24},{12,28},{16,0},{20,4},{24,8},{28,12},{1,17},{... | collective-permute-start | bytes 1572872 | tf_op jit(solution)/shard_map/ppermute | solution.py:128
  57.8 2.8 %pad_maximum_fusion = bf16[256,2,2048]{2,0,1:T(8,128)(2,1)} fusion(bf16[256,1,2048]{2,0,1:T(8,128)(2,1)} %bitcast.1, bf16[256,1,2048]{2,0,1:T(8,128)(2,1)S(1)} %copy-done.1), kind=kLoop, calls=%fused_computation.4 | loop fusion | flops 1048576 | bytes 4194304 | tf_op jit(solution)/shard_map/stack | solution.py:144
  60.6 2.8 %copy.6 = bf16[256,2,2048]{0,2,1:T(8,128)(2,1)S(1)} copy(bf16[256,2,2048]{2,0,1:T(8,128)(2,1)} %pad_maximum_fusion) | data formatting | bytes 4194304 | tf_op jit(solution)/shard_map/stack | solution.py:144
  63.4 0.7 convolution_bitcast_fusion
  64.1 4.4 %fusion.10 = f32[2,32,64]{2,1,0:T(8,128)S(1)} fusion(bf16[256,64,64]{0,2,1:T(8,128)(2,1)S(1)} %bitcast.117, bf16[2,32,64,256]{3,2,1,0:T(8,128)(2,1)S(1)} %bitcast.118), kind=kOutput, calls=%fused_computation.40 | convolution fusion | flops 134217728 | bytes 4210688 | tf_op jit(solution)/shard_map/noi,npi->op/dot_general | solution.py:20
  68.9 0.6 pad_maximum_fusion.3.x_ref
  69.6 19.4 %shard_map.28.x_ref = f32[2,64,64]{2,1,0:T(8,128)} custom-call(f32[2,64,64]{2,1,0:T(8,128)} %pad_maximum_fusion.3.x_ref), custom_call_target="tpu_custom_call" | custom-call | tf_op jit(solution)/shard_map/pallas_call | solution.py:61
  89.0 7.0 %shard_map.29 = bf16[2,64,64]{2,1,0:T(8,128)(2,1)} custom-call(f32[2,64,64]{2,1,0:T(8,128)} %shard_map.28.x_ref), custom_call_target="tpu_custom_call" | custom-call | tf_op jit(solution)/shard_map/pallas_call | solution.py:100
  96.1 0.7 slice.9
  97.1 1.5 fusion.62
  98.6 1.7 convert_bitcast_fusion.1
  100.3 1.2 copy.12
  101.5 2.1 %collective-permute-start.12 = (bf16[256,1024]{1,0:T(8,128)(2,1)}, bf16[256,1024]{1,0:T(8,128)(2,1)S(1)}, u32[]{:S(2)}, u32[]{:S(2)}) collective-permute-start(bf16[256,1024]{1,0:T(8,128)(2,1)} %get-tuple-element.13), channel_id=1, source_target_pairs={{0,16},{4,20},{8,24},{12,28},{16,0},{20,4},{24,8},{28,12},{1,17},{... | collective-permute-start | bytes 1572872 | tf_op jit(solution)/shard_map/ppermute | solution.py:128
  103.6 1.3 fusion.43
  104.9 1.0 collective-permute-start.17
  105.9 1.3 fusion.45
  107.3 1.4 fusion.57
  108.7 7.7 %collective-permute-done.12 = bf16[256,1024]{1,0:T(8,128)(2,1)S(1)} collective-permute-done((bf16[256,1024]{1,0:T(8,128)(2,1)}, bf16[256,1024]{1,0:T(8,128)(2,1)S(1)}, u32[]{:S(2)}, u32[]{:S(2)}) %collective-permute-start.12) | collective-permute-done | bytes 524320 | tf_op jit(solution)/shard_map/ppermute | solution.py:128
  116.7 1.8 %collective-permute-start.10 = (bf16[256,1024]{1,0:T(8,128)(2,1)}, bf16[256,1024]{1,0:T(8,128)(2,1)S(1)}, u32[]{:S(2)}, u32[]{:S(2)}) collective-permute-start(bf16[256,1024]{1,0:T(8,128)(2,1)} %collective-permute-done.3), channel_id=1, source_target_pairs={{0,16},{4,20},{8,24},{12,28},{16,0},{20,4},{24,8},{28,12},{1,17},{... | collective-permute-start | bytes 1572872 | tf_op jit(solution)/shard_map/ppermute | solution.py:128
  118.5 1.3 fusion.49
  120.2 1.3 fusion.51
  122.2 8.1 %collective-permute-done.17 = bf16[256,2048]{0,1:T(8,128)(2,1)S(1)} collective-permute-done((bf16[256,2048]{0,1:T(8,128)(2,1)S(1)}, bf16[256,2048]{0,1:T(8,128)(2,1)S(1)}, u32[]{:S(2)}, u32[]{:S(2)}) %collective-permute-start.17) | collective-permute-done | bytes 1048608 | tf_op jit(solution)/shard_map/ppermute | solution.py:125
  130.3 1.2 collective-permute-start.14
  131.7 0.6 copy-done.3
  132.3 0.8 fusion.61
  133.1 1.7 convert_bitcast_fusion
  134.8 1.2 copy.15
  136.0 1.4 fusion.21
  137.3 1.4 fusion.27
  138.7 1.4 fusion.23
  140.1 1.4 fusion.35
  141.8 0.5 collective-permute-start.11
  142.3 1.2 collective-permute-done.14
  145.5 1.4 fusion.29
  150.2 3.5 %collective-permute-start.18 = (bf16[256,512]{0,1:T(8,128)(2,1)S(1)}, bf16[256,512]{0,1:T(8,128)(2,1)S(1)}, u32[]{:S(2)}, u32[]{:S(2)}) collective-permute-start(bf16[256,512]{0,1:T(8,128)(2,1)S(1)} %select_convert_fusion), channel_id=1, source_target_pairs={{0,2},{1,3},{2,0},{3,1},{4,6},{5,7},{6,4},{7,5},{8,10},{9,11},{10,... | collective-permute-start | bytes 786440 | tf_op jit(solution)/shard_map/ppermute | solution.py:215
  154.5 17.6 %collective-permute-done.18 = bf16[256,512]{0,1:T(8,128)(2,1)S(1)} collective-permute-done((bf16[256,512]{0,1:T(8,128)(2,1)S(1)}, bf16[256,512]{0,1:T(8,128)(2,1)S(1)}, u32[]{:S(2)}, u32[]{:S(2)}) %collective-permute-start.18) | collective-permute-done | bytes 262176 | tf_op jit(solution)/shard_map/ppermute | solution.py:215
  172.2 5.3 %collective-permute-done.16 = bf16[256,512]{0,1:T(8,128)(2,1)S(1)} collective-permute-done((bf16[256,512]{0,1:T(8,128)(2,1)S(1)}, bf16[256,512]{0,1:T(8,128)(2,1)S(1)}, u32[]{:S(2)}, u32[]{:S(2)}) %collective-permute-start.16) | collective-permute-done | bytes 262176 | tf_op jit(solution)/shard_map/ppermute | solution.py:215
  178.3 1.0 pad_maximum_fusion.2
  (68 shorter events, 9.3 us)
Async XLA Ops:
  0.0 10.6 %collective-permute-start.1 = (bf16[512,1024]{1,0:T(8,128)(2,1)}, bf16[512,1024]{1,0:T(8,128)(2,1)S(1)}, u32[]{:S(2)}, u32[]{:S(2)}) collective-permute-start(bf16[512,1024]{1,0:T(8,128)(2,1)} %param.3), channel_id=1, source_target_pairs={{0,0},{1,1},{2,16},{3,17},{4,4},{5,5},{6,20},{7,21},{8,8},{9,9},{1... | collective-permute-start | bytes 3145736 | tf_op jit(solution)/shard_map/ppermute | solution.py:164
  5.0 27.6 %collective-permute-start = (bf16[256,2048]{1,0:T(8,128)(2,1)S(1)}, bf16[256,2048]{1,0:T(8,128)(2,1)}, u32[]{:S(2)}, u32[]{:S(2)}) collective-permute-start(bf16[256,2048]{1,0:T(8,128)(2,1)S(1)} %get-tuple-element.9), channel_id=1, source_target_pairs={{0,1},{1,0},{2,3},{3,2},{4,5},{5,4},{6,7},{7,6},{8,9},{9,8},{10,11... | collective-permute-start | bytes 3145736 | tf_op jit(solution)/shard_map/ppermute | solution.py:125
  10.6 47.2 %copy-start.1 = (bf16[256,1,2048]{2,0,1:T(8,128)(2,1)S(1)}, bf16[256,1,2048]{2,0,1:T(8,128)(2,1)}, u32[]{:S(2)}) copy-start(bf16[256,1,2048]{2,0,1:T(8,128)(2,1)} %get-tuple-element.8) | copy-start | bytes 3145732
  11.7 89.8 %collective-permute-start.3 = (bf16[256,1024]{1,0:T(8,128)(2,1)}, bf16[256,1024]{1,0:T(8,128)(2,1)}, u32[]{:S(2)}, u32[]{:S(2)}) collective-permute-start(bf16[256,1024]{1,0:T(8,128)(2,1)} %get-tuple-element.12), channel_id=1, source_target_pairs={{0,8},{4,12},{8,0},{12,4},{16,24},{20,28},{24,16},{28,20},{1,9},{5... | collective-permute-start | bytes 1572872 | tf_op jit(solution)/shard_map/ppermute | solution.py:128
  13.2 103.5 %collective-permute-start.2 = (bf16[256,1024]{1,0:T(8,128)(2,1)}, bf16[256,1024]{1,0:T(8,128)(2,1)}, u32[]{:S(2)}, u32[]{:S(2)}) collective-permute-start(bf16[256,1024]{1,0:T(8,128)(2,1)} %get-tuple-element.12), channel_id=1, source_target_pairs={{0,4},{4,0},{8,12},{12,8},{16,20},{20,16},{24,28},{28,24},{1,5},{5... | collective-permute-start | bytes 1572872 | tf_op jit(solution)/shard_map/ppermute | solution.py:128
  13.2 106.7 %collective-permute-start.5 = (bf16[256,1024]{1,0:T(8,128)(2,1)}, bf16[256,1024]{1,0:T(8,128)(2,1)}, u32[]{:S(2)}, u32[]{:S(2)}) collective-permute-start(bf16[256,1024]{1,0:T(8,128)(2,1)} %get-tuple-element.13), channel_id=1, source_target_pairs={{0,4},{4,0},{8,12},{12,8},{16,20},{20,16},{24,28},{28,24},{1,5},{5... | collective-permute-start | bytes 1572872 | tf_op jit(solution)/shard_map/ppermute | solution.py:128
  13.7 91.2 %collective-permute-start.6 = (bf16[256,1024]{1,0:T(8,128)(2,1)}, bf16[256,1024]{1,0:T(8,128)(2,1)}, u32[]{:S(2)}, u32[]{:S(2)}) collective-permute-start(bf16[256,1024]{1,0:T(8,128)(2,1)} %get-tuple-element.13), channel_id=1, source_target_pairs={{0,8},{4,12},{8,0},{12,4},{16,24},{20,28},{24,16},{28,20},{1,9},{5... | collective-permute-start | bytes 1572872 | tf_op jit(solution)/shard_map/ppermute | solution.py:128
  32.6 74.7 %collective-permute-start.8 = (bf16[256,1024]{1,0:T(8,128)(2,1)}, bf16[256,1024]{1,0:T(8,128)(2,1)}, u32[]{:S(2)}, u32[]{:S(2)}) collective-permute-start(bf16[256,1024]{1,0:T(8,128)(2,1)} %get-tuple-element.12), channel_id=1, source_target_pairs={{0,16},{4,20},{8,24},{12,28},{16,0},{20,4},{24,8},{28,12},{1,17},{... | collective-permute-start | bytes 1572872 | tf_op jit(solution)/shard_map/ppermute | solution.py:128
  100.3 4.6 %copy-start.2 = (bf16[256,2048]{0,1:T(8,128)(2,1)S(1)}, bf16[256,2048]{0,1:T(8,128)(2,1)}, u32[]{:S(2)}) copy-start(bf16[256,2048]{0,1:T(8,128)(2,1)} %copy.21) | copy-start | bytes 3145732
  101.5 14.9 %collective-permute-start.12 = (bf16[256,1024]{1,0:T(8,128)(2,1)}, bf16[256,1024]{1,0:T(8,128)(2,1)S(1)}, u32[]{:S(2)}, u32[]{:S(2)}) collective-permute-start(bf16[256,1024]{1,0:T(8,128)(2,1)} %get-tuple-element.13), channel_id=1, source_target_pairs={{0,16},{4,20},{8,24},{12,28},{16,0},{20,4},{24,8},{28,12},{1,17},{... | collective-permute-start | bytes 1572872 | tf_op jit(solution)/shard_map/ppermute | solution.py:128
  104.9 25.4 %collective-permute-start.17 = (bf16[256,2048]{0,1:T(8,128)(2,1)S(1)}, bf16[256,2048]{0,1:T(8,128)(2,1)S(1)}, u32[]{:S(2)}, u32[]{:S(2)}) collective-permute-start(bf16[256,2048]{0,1:T(8,128)(2,1)S(1)} %copy-done.2), channel_id=1, source_target_pairs={{0,1},{1,0},{2,3},{3,2},{4,5},{5,4},{6,7},{7,6},{8,9},{9,8},{10,11... | collective-permute-start | bytes 3145736 | tf_op jit(solution)/shard_map/ppermute | solution.py:125
  107.3 37.9 %collective-permute-start.4 = (bf16[256,1024]{1,0:T(8,128)(2,1)}, bf16[256,1024]{1,0:T(8,128)(2,1)S(1)}, u32[]{:S(2)}, u32[]{:S(2)}) collective-permute-start(bf16[256,1024]{1,0:T(8,128)(2,1)} %collective-permute-done.3), channel_id=1, source_target_pairs={{0,4},{4,0},{8,12},{12,8},{16,20},{20,16},{24,28},{28,24},{1,5},{5... | collective-permute-start | bytes 1572872 | tf_op jit(solution)/shard_map/ppermute | solution.py:128
  116.4 25.4 %collective-permute-start.9 = (bf16[256,1024]{1,0:T(8,128)(2,1)}, bf16[256,1024]{1,0:T(8,128)(2,1)S(1)}, u32[]{:S(2)}, u32[]{:S(2)}) collective-permute-start(bf16[256,1024]{1,0:T(8,128)(2,1)} %collective-permute-done.8), channel_id=1, source_target_pairs={{0,4},{4,0},{8,12},{12,8},{16,20},{20,16},{24,28},{28,24},{1,5},{5... | collective-permute-start | bytes 1572872 | tf_op jit(solution)/shard_map/ppermute | solution.py:128
  116.7 25.1 %collective-permute-start.10 = (bf16[256,1024]{1,0:T(8,128)(2,1)}, bf16[256,1024]{1,0:T(8,128)(2,1)S(1)}, u32[]{:S(2)}, u32[]{:S(2)}) collective-permute-start(bf16[256,1024]{1,0:T(8,128)(2,1)} %collective-permute-done.3), channel_id=1, source_target_pairs={{0,16},{4,20},{8,24},{12,28},{16,0},{20,4},{24,8},{28,12},{1,17},{... | collective-permute-start | bytes 1572872 | tf_op jit(solution)/shard_map/ppermute | solution.py:128
  119.9 24.3 %collective-permute-start.13 = (bf16[256,1024]{1,0:T(8,128)(2,1)S(1)}, bf16[256,1024]{1,0:T(8,128)(2,1)S(1)}, u32[]{:S(2)}, u32[]{:S(2)}) collective-permute-start(bf16[256,1024]{1,0:T(8,128)(2,1)S(1)} %collective-permute-done.12), channel_id=1, source_target_pairs={{0,4},{4,0},{8,12},{12,8},{16,20},{20,16},{24,28},{28,24},{1,5},{5... | collective-permute-start | bytes 1572872 | tf_op jit(solution)/shard_map/ppermute | solution.py:128
  121.5 10.0 %copy-start = (bf16[256,2048]{0,1:T(8,128)(2,1)S(1)}, bf16[256,2048]{0,1:T(8,128)(2,1)}, u32[]{:S(2)}) copy-start(bf16[256,2048]{0,1:T(8,128)(2,1)} %copy.13) | copy-start | bytes 3145732
  130.3 13.2 %collective-permute-start.14 = (bf16[256,1024]{1,0:T(8,128)(2,1)S(1)}, bf16[256,1024]{1,0:T(8,128)(2,1)S(1)}, u32[]{:S(2)}, u32[]{:S(2)}) collective-permute-start(bf16[256,1024]{1,0:T(8,128)(2,1)S(1)} %collective-permute-done.12), channel_id=1, source_target_pairs={{0,8},{4,12},{8,0},{12,4},{16,24},{20,28},{24,16},{28,20},{1,9},{5... | collective-permute-start | bytes 1572872 | tf_op jit(solution)/shard_map/ppermute | solution.py:128
  131.5 0.8 copy-start.3
  141.7 5.7 %collective-permute-start.7 = (bf16[256,1024]{1,0:T(8,128)(2,1)}, bf16[256,1024]{1,0:T(8,128)(2,1)S(1)}, u32[]{:S(2)}, u32[]{:S(2)}) collective-permute-start(bf16[256,1024]{1,0:T(8,128)(2,1)} %collective-permute-done.6), channel_id=1, source_target_pairs={{0,4},{4,0},{8,12},{12,8},{16,20},{20,16},{24,28},{28,24},{1,5},{5... | collective-permute-start | bytes 1572872 | tf_op jit(solution)/shard_map/ppermute | solution.py:128
  141.8 7.6 %collective-permute-start.11 = (bf16[256,1024]{1,0:T(8,128)(2,1)S(1)}, bf16[256,1024]{1,0:T(8,128)(2,1)S(1)}, u32[]{:S(2)}, u32[]{:S(2)}) collective-permute-start(bf16[256,1024]{1,0:T(8,128)(2,1)S(1)} %collective-permute-done.10), channel_id=1, source_target_pairs={{0,4},{4,0},{8,12},{12,8},{16,20},{20,16},{24,28},{28,24},{1,5},{5... | collective-permute-start | bytes 1572872 | tf_op jit(solution)/shard_map/ppermute | solution.py:128
  143.5 6.3 %collective-permute-start.15 = (bf16[256,1024]{1,0:T(8,128)(2,1)S(1)}, bf16[256,1024]{1,0:T(8,128)(2,1)S(1)}, u32[]{:S(2)}, u32[]{:S(2)}) collective-permute-start(bf16[256,1024]{1,0:T(8,128)(2,1)S(1)} %collective-permute-done.14), channel_id=1, source_target_pairs={{0,4},{4,0},{8,12},{12,8},{16,20},{20,16},{24,28},{28,24},{1,5},{5... | collective-permute-start | bytes 1572872 | tf_op jit(solution)/shard_map/ppermute | solution.py:128
  150.2 21.9 %collective-permute-start.18 = (bf16[256,512]{0,1:T(8,128)(2,1)S(1)}, bf16[256,512]{0,1:T(8,128)(2,1)S(1)}, u32[]{:S(2)}, u32[]{:S(2)}) collective-permute-start(bf16[256,512]{0,1:T(8,128)(2,1)S(1)} %select_convert_fusion), channel_id=1, source_target_pairs={{0,2},{1,3},{2,0},{3,1},{4,6},{5,7},{6,4},{7,5},{8,10},{9,11},{10,... | collective-permute-start | bytes 786440 | tf_op jit(solution)/shard_map/ppermute | solution.py:215
  154.4 23.1 %collective-permute-start.16 = (bf16[256,512]{0,1:T(8,128)(2,1)S(1)}, bf16[256,512]{0,1:T(8,128)(2,1)S(1)}, u32[]{:S(2)}, u32[]{:S(2)}) collective-permute-start(bf16[256,512]{0,1:T(8,128)(2,1)S(1)} %select_convert_fusion.1), channel_id=1, source_target_pairs={{0,2},{1,3},{2,0},{3,1},{4,6},{5,7},{6,4},{7,5},{8,10},{9,11},{10,... | collective-permute-start | bytes 786440 | tf_op jit(solution)/shard_map/ppermute | solution.py:215

commit v2 on v1

--- a/solution.py
+++ b/solution.py
@@ -163,23 +163,18 @@
                 swaps.append((r * cols + c, r * cols + c))
     own_query = lax.ppermute(query_grads, ("row", "col"), swaps)
     query_count, query_width = query_grads.shape
-    bits = [1 << k for k in range(1, rows.bit_length() - 1)]
-    held = []
-    for number, piece in enumerate(jnp.split(own_query, 2, axis=0)):
-        by_offset = {0: piece}
-        near_core = {}
-        for bit in (bits if number == 0 else bits[::-1]):
-            arrived = {d ^ bit: across(v, bit) for d, v in by_offset.items()}
-            by_offset.update(arrived)
-        for d, value in by_offset.items():
-            near_core[d ^ 1] = across(value, 1)
-        by_offset.update(near_core)
-        held.append(by_offset)
+    parity = [[r for r in range(rows) if r % 2 == core] for core in range(2)]
+    own_query, _ = lax.optimization_barrier((own_query, ready))
+    own_core = lax.all_gather(own_query, "row", axis=0, axis_index_groups=parity)
+    own_core, inverses = lax.optimization_barrier((own_core, inverses))
+    other_core = across(own_core, 1)
+    pair_count = half_rows // 2
+    held = [v.reshape(LAYERS, pair_count, query_count, query_width) for v in (own_core, other_core)]
+    core = lax.rem(row, 2)
 
     scale = 1.0 / math.sqrt(LAYERS * PROJ * PROJ)
     output_inverse = to_order(inverses[1], 1)
-    own_side = lax.div(row, half_rows) == layer
-    quarter = lax.rem(row, half_rows)
+    own_side = layer == 0
     pairs = [(c, (c + group) % cols) for c in range(cols)]
     results = []
     for turn in turns:
@@ -190,26 +185,17 @@
             "op,npj->noj", output_inverse, half, preferred_element_type=jnp.float32
         ).astype(jnp.bfloat16)
         conditioned = conditioned.reshape(part, PROJ * PROJ)
-        columns = [
-            lax.dynamic_slice_in_dim(conditioned, (quarter ^ d) * query_width, query_width, 1)
-            for d in range(half_rows)
-        ]
-        sides = []
-        for side in range(LAYERS):
-            products = []
-            for by_offset in held:
-                products.append(
-                    sum(
-                        lax.dot_general(
-                            columns[d],
-                            by_offset[side * half_rows + d],
-                            (((1,), (1,)), ((), ())),
-                            preferred_element_type=jnp.float32,
-                        )
-                        for d in range(half_rows)
-                    )
-                )
-            sides.append(jnp.concatenate(products, axis=1) * scale)
+        by_core = conditioned.reshape(part, pair_count, 2, query_width)
+        product = sum(
+            jnp.einsum(
+                "nqf,sqmf->snm",
+                lax.dynamic_index_in_dim(by_core, core ^ e, 2, keepdims=False),
+                held[e],
+                preferred_element_type=jnp.float32,
+            )
+            for e in range(2)
+        )
+        sides = product * scale
         kept = jnp.where(own_side, sides[0], sides[1])
         given = jnp.where(own_side, sides[1], sides[0]).astype(jnp.bfloat16)
         results.append(kept + lax.ppermute(given, "col", pairs).astype(jnp.float32))

time: 180 us -> 215 us (1.19)
  waiting for transfers between devices: 58.3 us -> 114 us
  starting transfers between devices: 43.2 us -> 8.29 us
  between operations: 0.57 us -> 13.6 us
  matrix products: 31.2 us -> 21.2 us
  Pallas kernels: 26.5 us -> 34.4 us
  other arithmetic: 5.29 us -> 8.28 us
    ppermute x2, waiting for transfers between devices: 26.5 us -> 65 us  [shifted(): return lax.ppermute(value, 'col', pairs)]
    ppermute x14 -> x1, starting transfers between devices: 33.8 us -> 0.01 us  [across(): return lax.ppermute(value, 'row', [(r, r ^ bit) for r in range(rows)])]
    all_gather x0 -> x1, waiting for transfers between devices: none -> 29.6 us  [local(): lax.all_gather(own_query, 'row', axis=0, axis_index_groups=parity)]
    dot_general x32 -> x4, matrix products: 20.5 us -> 9.56 us  [local(): jnp.einsum('nqf,sqmf->snm', lax.dynamic_index_in_dim(by_core, core ^ e, 2...]
    ppermute x14 -> x1, waiting for transfers between devices: 8.89 us -> 0.01 us  [across(): return lax.ppermute(value, 'row', [(r, r ^ bit) for r in range(rows)])]
    pallas_call x1, Pallas kernels: 19.4 us -> 27.3 us  [sum_over_group(): pl.pallas_call(functools.partial(sum_kernel, rows, group), out_shape=jax....]
    ppermute x2, waiting for transfers between devices: 22.9 us -> 19 us  [local(): results.append(kept + lax.ppermute(given, 'col', pairs).astype(jnp.float32))]
    another operation x2, other arithmetic: 2.95 us -> 5.91 us  [local(): turns.append(jnp.stack(pieces, axis=1))]
  transfers between devices with their start and end apart: 19 -> 7, of which waited for: 6 -> 5; matrix products, arithmetic and copies ran while one was open for 27% -> 16% of each run, Pallas kernels for 15% -> 16%
where the time goes in v2:
time: 215 us
  waiting for transfers between devices  114 us (53%)
  Pallas kernels  34.4 us (16%)
  matrix products  21.2 us (10%)
  local copies, waits for them, and re-layouts  15.6 us (7%)
  between operations  13.6 us (6%)
  starting transfers between devices  8.29 us (4%)
  other arithmetic  8.28 us (4%)
    ppermute x2, waiting for transfers between devices, shifted(): return lax.ppermute(value, 'col', pairs)  65 us
    all_gather x1, waiting for transfers between devices, local(): lax.all_gather(own_query, 'row', axis=0, axis_index_groups=parity)  29.6 us
    pallas_call x1, Pallas kernels, sum_over_group(): pl.pallas_call(functools.partial(sum_kernel, rows, group), out_shape=jax....  27.3 us
    ppermute x2, waiting for transfers between devices, local(): results.append(kept + lax.ppermute(given, 'col', pairs).astype(jnp.float32))  19 us
    dot_general x4, matrix products, local(): jnp.einsum('nqf,sqmf->snm', lax.dynamic_index_in_dim(by_core, core ^ e, 2...  9.56 us
    pallas_call x1, Pallas kernels, invert(): pl.pallas_call(functools.partial(invert_kernel, scale), out_shape=jax.Sha...  7.04 us
    another operation x2, other arithmetic, local(): turns.append(jnp.stack(pieces, axis=1))  5.91 us
    dynamic_slice x2, local copies, waits for them, and re-layouts, chunk(): lax.dynamic_slice_in_dim(train_grads, lax.rem(index, group) * part, part, 0)  4.63 us
  transfers between devices with their start and end apart: 7, of which 5 were waited for; matrix products, arithmetic and copies ran while one was open for 16% of the time, Pallas kernels for 16%

profile of v2, /device:TPU:0, one launch (start us, length us, event | category | flops | bytes accessed | tf_op | source)
XLA Modules:
  0.0 215.0 jit_solution(1876293701194398426)
XLA Ops:
  6.5 3.3 %constant_dynamic-slice_fusion = (bf16[256,2048]{1,0:T(8,128)(2,1)}, bf16[256,2048]{1,0:T(8,128)(2,1)S(1)}, bf16[256,1,2048]{2,0,1:T(8,128)(2,1)S(1)}) fusion(bf16[512,2048]{1,0:T(8,128)(2,1)} %param.2, s32[]{:T(128)S(6)} %select_n.77, s32[]{:T(128)S(6)} %select_n.68, s32[]{:T(128)S(6)} %select_n.69), kind=kLoop, calls=%fused_computation.65 | loop fusion | bytes 6291468 | tf_op jit(solution)/shard_map/dynamic_slice | solution.py:131
  9.8 3.0 %collective-permute-start.1 = (bf16[256,2048]{1,0:T(8,128)(2,1)S(1)}, bf16[256,2048]{1,0:T(8,128)(2,1)S(1)}, u32[]{:S(2)}, u32[]{:S(2)}) collective-permute-start(bf16[256,2048]{1,0:T(8,128)(2,1)S(1)} %get-tuple-element.14), channel_id=1, source_target_pairs={{0,1},{1,0},{2,3},{3,2},{4,5},{5,4},{6,7},{7,6},{8,9},{9,8},{10,11... | collective-permute-start | bytes 3145736 | tf_op jit(solution)/shard_map/ppermute | solution.py:125
  12.9 0.7 collective-permute-start
  13.6 41.9 %collective-permute-done.1 = bf16[256,2048]{1,0:T(8,128)(2,1)S(1)} collective-permute-done((bf16[256,2048]{1,0:T(8,128)(2,1)S(1)}, bf16[256,2048]{1,0:T(8,128)(2,1)S(1)}, u32[]{:S(2)}, u32[]{:S(2)}) %collective-permute-start.1) | collective-permute-done | bytes 1048608 | tf_op jit(solution)/shard_map/ppermute | solution.py:125
  55.5 1.0 copy-done.1
  56.5 1.0 copy-done
  57.5 0.0 all-gather.3.cloned.1.call-update
  57.5 2.8 %pad_maximum_fusion = bf16[256,2,2048]{2,0,1:T(8,128)(2,1)} fusion(bf16[256,1,2048]{2,0,1:T(8,128)(2,1)} %bitcast.136, bf16[256,1,2048]{2,0,1:T(8,128)(2,1)S(1)} %get-tuple-element.15), kind=kLoop, calls=%fused_computation.4 | loop fusion | flops 1048576 | bytes 4194304 | tf_op jit(solution)/shard_map/stack | solution.py:144
  60.3 2.8 %copy.6 = bf16[256,2,2048]{0,2,1:T(8,128)(2,1)S(1)} copy(bf16[256,2,2048]{2,0,1:T(8,128)(2,1)} %pad_maximum_fusion) | data formatting | bytes 4194304 | tf_op jit(solution)/shard_map/stack | solution.py:144
  63.2 4.4 %fusion.12 = f32[2,32,64]{2,1,0:T(8,128)S(1)} fusion(bf16[256,64,64]{0,2,1:T(8,128)(2,1)S(1)} %bitcast.126, bf16[2,32,64,256]{3,2,1,0:T(8,128)(2,1)S(1)} %bitcast.127), kind=kOutput, calls=%fused_computation.26 | convolution fusion | flops 134217728 | bytes 4210688 | tf_op jit(solution)/shard_map/noi,npi->op/dot_general | solution.py:20
  67.6 0.1 concatenate.17
  67.7 0.1 concatenate.18
  67.8 0.1 constant_dynamic-slice_fusion.2
  67.9 0.1 maximum_bitcast_fusion
  68.0 0.7 convolution_bitcast_fusion.4
  68.7 0.6 pad_maximum_fusion.3.x_ref
  69.3 27.3 %shard_map.28.x_ref = f32[2,64,64]{2,1,0:T(8,128)} custom-call(f32[2,64,64]{2,1,0:T(8,128)} %pad_maximum_fusion.3.x_ref), custom_call_target="tpu_custom_call" | custom-call | tf_op jit(solution)/shard_map/pallas_call | solution.py:61
  96.6 7.0 %shard_map.29 = bf16[2,64,64]{2,1,0:T(8,128)(2,1)} custom-call(f32[2,64,64]{2,1,0:T(8,128)} %shard_map.28.x_ref), custom_call_target="tpu_custom_call" | custom-call | tf_op jit(solution)/shard_map/pallas_call | solution.py:100
  103.7 29.6 %all-gather.3.cloned.1.call-done = bf16[2048,1024]{1,0:T(8,128)(2,1)} async-done(((bf16[512,1024]{1,0:T(8,128)(2,1)}), bf16[2048,1024]{1,0:T(8,128)(2,1)}) %all-gather.3.cloned.1.call-update) | async-done | bytes 4194320 | tf_op jit(solution)/shard_map/all_gather | solution.py:168
  133.2 2.3 %copy.27 = bf16[256,2048]{0,1:T(8,128)(2,1)} copy(bf16[256,2048]{1,0:T(8,128)(2,1)} %get-tuple-element.13) | data formatting | bytes 2097152 | tf_op jit(solution)/shard_map/optimization_barrier | solution.py:140
  135.5 1.5 collective-permute-start.4
  137.0 1.3 copy.15
  138.3 23.1 %collective-permute-done.4 = bf16[256,2048]{0,1:T(8,128)(2,1)} collective-permute-done((bf16[256,2048]{0,1:T(8,128)(2,1)}, bf16[256,2048]{0,1:T(8,128)(2,1)}, u32[]{:S(2)}, u32[]{:S(2)}) %collective-permute-start.4) | collective-permute-done | bytes 1048608 | tf_op jit(solution)/shard_map/ppermute | solution.py:125
  161.4 3.1 %pad_maximum_fusion.1 = bf16[256,2,2048]{0,2,1:T(8,128)(2,1)} fusion(bf16[256,1,2048]{0,2,1:T(8,128)(2,1)} %bitcast.37, bf16[256,1,2048]{0,2,1:T(8,128)(2,1)} %bitcast.131), kind=kLoop, calls=%fused_computation.5 | loop fusion | flops 1048576 | bytes 4194304 | tf_op jit(solution)/shard_map/stack | solution.py:144
  164.5 0.1 copy.9
  164.6 0.1 copy.10
  164.7 0.1 copy.11
  164.8 2.3 %fusion.33 = bf16[256,64,64]{0,2,1:T(8,128)(2,1)S(1)} fusion(bf16[256,64,64]{0,2,1:T(8,128)(2,1)} %bitcast.130, bf16[2,64,64]{2,1,0:T(8,128)(2,1)S(1)} %copy-done.2), kind=kOutput, calls=%fused_computation.53 | convolution fusion | flops 134217728 | bytes 4210688 | tf_op jit(solution)/shard_map/noi,ij->noj/dot_general | solution.py:181
  167.2 1.7 convert_bitcast_fusion
  168.9 1.2 copy.17
  170.1 0.7 fusion.35
  170.8 1.7 convert_bitcast_fusion.1
  172.6 1.2 copy.12
  173.8 1.0 copy-done.3
  174.8 1.3 convolution_bitcast_fusion.1
  176.1 1.3 convolution_bitcast_fusion.3
  177.4 3.5 %fusion.11 = f32[2,256,512]{2,1,0:T(8,128)S(1)} fusion(f32[2,512,256]{1,2,0:T(8,128)S(1)} %convolution_bitcast_fusion.1, bf16[2,2,512,1024]{3,2,1,0:T(8,128)(2,1)} %bitcast.27, bf16[256,2,2,1024]{0,3,2,1:T(8,128)(2,1)S(1)} %bitcast.135, s32[]{:T(128)S(6)} %select_n.73), kind=kOutput, calls=%fused_computation.21 | convolution fusion | flops 1074266112 | bytes 7340036 | tf_op jit(solution)/shard_map/nqf,sqmf->snm/dot_general | solution.py:190
  180.9 0.1 fusion.32
  180.9 2.5 %collective-permute-start.5 = (bf16[256,512]{1,0:T(8,128)(2,1)S(1)}, bf16[256,512]{1,0:T(8,128)(2,1)S(1)}, u32[]{:S(2)}, u32[]{:S(2)}) collective-permute-start(bf16[256,512]{1,0:T(8,128)(2,1)S(1)} %fusion.32), channel_id=1, source_target_pairs={{0,2},{1,3},{2,0},{3,1},{4,6},{5,7},{6,4},{7,5},{8,10},{9,11},{10,... | collective-permute-start | bytes 786440 | tf_op jit(solution)/shard_map/ppermute | solution.py:201
  183.4 3.5 %fusion.8 = f32[2,256,512]{2,1,0:T(8,128)S(1)} fusion(f32[2,512,256]{1,2,0:T(8,128)S(1)} %convolution_bitcast_fusion.3, bf16[2,2,512,1024]{3,2,1,0:T(8,128)(2,1)} %bitcast.27, bf16[256,2,2,1024]{0,3,2,1:T(8,128)(2,1)S(1)} %bitcast.133, s32[]{:T(128)S(6)} %select_n.73), kind=kOutput, calls=%fused_computation.18 | convolution fusion | flops 1074266112 | bytes 7340036 | tf_op jit(solution)/shard_map/nqf,sqmf->snm/dot_general | solution.py:190
  186.9 0.1 fusion.31
  186.9 0.6 collective-permute-start.3
  187.5 14.6 %collective-permute-done.5 = bf16[256,512]{1,0:T(8,128)(2,1)S(1)} collective-permute-done((bf16[256,512]{1,0:T(8,128)(2,1)S(1)}, bf16[256,512]{1,0:T(8,128)(2,1)S(1)}, u32[]{:S(2)}, u32[]{:S(2)}) %collective-permute-start.5) | collective-permute-done | bytes 262176 | tf_op jit(solution)/shard_map/ppermute | solution.py:201
  202.1 0.1 fusion.29
  202.2 4.4 %collective-permute-done.3 = bf16[256,512]{1,0:T(8,128)(2,1)S(1)} collective-permute-done((bf16[256,512]{1,0:T(8,128)(2,1)S(1)}, bf16[256,512]{1,0:T(8,128)(2,1)S(1)}, u32[]{:S(2)}, u32[]{:S(2)}) %collective-permute-start.3) | collective-permute-done | bytes 262176 | tf_op jit(solution)/shard_map/ppermute | solution.py:201
  206.7 0.1 fusion.30
  206.8 0.3 fusion.28
  207.1 1.0 pad_maximum_fusion.2
  (17 shorter events, 0.1 us)
Async XLA Ops:
  6.5 126.7 %all-gather.3.cloned.1.call-start = ((), (), s32[]{:S(2)}) async-start(), calls=%async_computation | async-start | bytes 5242880 | tf_op jit(solution)/shard_map/all_gather | solution.py:168
  6.5 6.3 %copy-start.4 = (bf16[512,1024]{1,0:T(8,128)(2,1)S(1)}, bf16[512,1024]{1,0:T(8,128)(2,1)}, u32[]{:S(2)}) copy-start(bf16[512,1024]{1,0:T(8,128)(2,1)} %param.3) | copy-start | bytes 3145732
  9.8 45.7 %collective-permute-start.1 = (bf16[256,2048]{1,0:T(8,128)(2,1)S(1)}, bf16[256,2048]{1,0:T(8,128)(2,1)S(1)}, u32[]{:S(2)}, u32[]{:S(2)}) collective-permute-start(bf16[256,2048]{1,0:T(8,128)(2,1)S(1)} %get-tuple-element.14), channel_id=1, source_target_pairs={{0,1},{1,0},{2,3},{3,2},{4,5},{5,4},{6,7},{7,6},{8,9},{9,8},{10,11... | collective-permute-start | bytes 3145736 | tf_op jit(solution)/shard_map/ppermute | solution.py:125
  12.9 43.6 %collective-permute-start = (bf16[512,1024]{1,0:T(8,128)(2,1)S(1)}, bf16[512,1024]{1,0:T(8,128)(2,1)S(1)}, u32[]{:S(2)}, u32[]{:S(2)}) collective-permute-start(bf16[512,1024]{1,0:T(8,128)(2,1)S(1)} %copy-done.4), channel_id=1, source_target_pairs={{0,0},{1,1},{2,16},{3,17},{4,4},{5,5},{6,20},{7,21},{8,8},{9,9},{1... | collective-permute-start | bytes 3145736 | tf_op jit(solution)/shard_map/ppermute | solution.py:164
  55.5 1.0 copy-start.1
  56.5 1.0 copy-start
  133.2 44.1 %collective-permute-start.2 = (bf16[4,512,1024]{2,1,0:T(8,128)(2,1)}, bf16[4,512,1024]{2,1,0:T(8,128)(2,1)}, u32[]{:S(2)}, u32[]{:S(2)}) collective-permute-start(bf16[4,512,1024]{2,1,0:T(8,128)(2,1)} %bitcast.140), channel_id=1, source_target_pairs={{0,4},{4,0},{8,12},{12,8},{16,20},{20,16},{24,28},{28,24},{1,5},{5... | collective-permute-start | bytes 12582920 | tf_op jit(solution)/shard_map/ppermute | solution.py:128
  135.5 25.9 %collective-permute-start.4 = (bf16[256,2048]{0,1:T(8,128)(2,1)}, bf16[256,2048]{0,1:T(8,128)(2,1)}, u32[]{:S(2)}, u32[]{:S(2)}) collective-permute-start(bf16[256,2048]{0,1:T(8,128)(2,1)} %copy.27), channel_id=1, source_target_pairs={{0,1},{1,0},{2,3},{3,2},{4,5},{5,4},{6,7},{7,6},{8,9},{9,8},{10,11... | collective-permute-start | bytes 3145736 | tf_op jit(solution)/shard_map/ppermute | solution.py:125
  161.4 3.1 %slice-start = ((bf16[2,64,64]{2,1,0:T(8,128)(2,1)}), bf16[1,64,64]{2,1,0:T(8,128)(2,1)S(1)}, s32[]{:S(2)}) async-start(bf16[2,64,64]{2,1,0:T(8,128)(2,1)} %shard_map.29), calls=%async_computation.1 | async-start | bytes 32768 | tf_op jit(solution)/shard_map/slice | solution.py:176
  161.4 3.4 %copy-start.2 = (bf16[2,64,64]{2,1,0:T(8,128)(2,1)S(1)}, bf16[2,64,64]{2,1,0:T(8,128)(2,1)}, u32[]{:S(2)}) copy-start(bf16[2,64,64]{2,1,0:T(8,128)(2,1)} %shard_map.29) | copy-start | bytes 49156
  172.6 2.2 %copy-start.3 = (bf16[2048,1024]{1,0:T(8,128)(2,1)S(1)}, bf16[2048,1024]{1,0:T(8,128)(2,1)}, u32[]{:S(2)}) copy-start(bf16[2048,1024]{1,0:T(8,128)(2,1)} %all-gather.3.cloned.1.call-done) | copy-start | bytes 12582916
  180.9 21.2 %collective-permute-start.5 = (bf16[256,512]{1,0:T(8,128)(2,1)S(1)}, bf16[256,512]{1,0:T(8,128)(2,1)S(1)}, u32[]{:S(2)}, u32[]{:S(2)}) collective-permute-start(bf16[256,512]{1,0:T(8,128)(2,1)S(1)} %fusion.32), channel_id=1, source_target_pairs={{0,2},{1,3},{2,0},{3,1},{4,6},{5,7},{6,4},{7,5},{8,10},{9,11},{10,... | collective-permute-start | bytes 786440 | tf_op jit(solution)/shard_map/ppermute | solution.py:201
  186.9 19.7 %collective-permute-start.3 = (bf16[256,512]{1,0:T(8,128)(2,1)S(1)}, bf16[256,512]{1,0:T(8,128)(2,1)S(1)}, u32[]{:S(2)}, u32[]{:S(2)}) collective-permute-start(bf16[256,512]{1,0:T(8,128)(2,1)S(1)} %fusion.31), channel_id=1, source_target_pairs={{0,2},{1,3},{2,0},{3,1},{4,6},{5,7},{6,4},{7,5},{8,10},{9,11},{10,... | collective-permute-start | bytes 786440 | tf_op jit(solution)/shard_map/ppermute | solution.py:201
Sparse Core Ops, SparseCore 0:
  57.6 75.5 all-gather.2

commit v3 on v2

--- a/solution.py
+++ b/solution.py
@@ -124,23 +124,15 @@
         pairs = [(c, c // group * group + (c + step) % group) for c in range(cols)]
         return lax.ppermute(value, "col", pairs)
 
-    def across(value, bit):
-        return lax.ppermute(value, "row", [(r, r ^ bit) for r in range(rows)])
-
     def chunk(index):
         return lax.dynamic_slice_in_dim(train_grads, lax.rem(index, group) * part, part, 0)
 
     turns = []
-    ready = None
     for k in range(group):
         pieces = [chunk(place + k)]
         for step in range(1, group):
             sent = chunk(place + step + k)
-            if ready is not None:
-                sent, _ = lax.optimization_barrier((sent, ready))
             pieces.append(shifted(sent, step))
-        if k == 0:
-            ready = pieces[-1]
         turns.append(jnp.stack(pieces, axis=1))
 
     def to_order(value, axis):
@@ -164,13 +156,8 @@
     own_query = lax.ppermute(query_grads, ("row", "col"), swaps)
     query_count, query_width = query_grads.shape
     parity = [[r for r in range(rows) if r % 2 == core] for core in range(2)]
-    own_query, _ = lax.optimization_barrier((own_query, ready))
-    own_core = lax.all_gather(own_query, "row", axis=0, axis_index_groups=parity)
-    own_core, inverses = lax.optimization_barrier((own_core, inverses))
-    other_core = across(own_core, 1)
-    pair_count = half_rows // 2
-    held = [v.reshape(LAYERS, pair_count, query_count, query_width) for v in (own_core, other_core)]
-    core = lax.rem(row, 2)
+    queries = lax.all_gather(own_query, "row", axis=0)
+    queries = queries.reshape(LAYERS, half_rows, query_count, query_width)
 
     scale = 1.0 / math.sqrt(LAYERS * PROJ * PROJ)
     output_inverse = to_order(inverses[1], 1)
@@ -185,15 +172,11 @@
             "op,npj->noj", output_inverse, half, preferred_element_type=jnp.float32
         ).astype(jnp.bfloat16)
         conditioned = conditioned.reshape(part, PROJ * PROJ)
-        by_core = conditioned.reshape(part, pair_count, 2, query_width)
-        product = sum(
-            jnp.einsum(
-                "nqf,sqmf->snm",
-                lax.dynamic_index_in_dim(by_core, core ^ e, 2, keepdims=False),
-                held[e],
-                preferred_element_type=jnp.float32,
-            )
-            for e in range(2)
+        product = jnp.einsum(
+            "nqf,sqmf->snm",
+            conditioned.reshape(part, half_rows, query_width),
+            queries,
+            preferred_element_type=jnp.float32,
         )
         sides = product * scale
         kept = jnp.where(own_side, sides[0], sides[1])

time: 215 us -> 184 us (0.86)
  waiting for transfers between devices: 114 us -> 64.2 us
  Pallas kernels: 34.4 us -> 57.2 us
  matrix products: 21.2 us -> 18.5 us
    all_gather x1, waiting for transfers between devices: 29.6 us -> 0.01 us  [local(): queries = lax.all_gather(own_query, 'row', axis=0)]
    pallas_call x1, Pallas kernels: 27.3 us -> 50.1 us  [sum_over_group(): pl.pallas_call(functools.partial(sum_kernel, rows, group), out_shape=jax....]
    ppermute x2, waiting for transfers between devices: 65 us -> 43.6 us  [shifted(): return lax.ppermute(value, 'col', pairs)]
    convert_element_type x2, local copies, waits for them, and re-layouts: 2.37 us -> 5.11 us  [local(): conditioned = jnp.einsum('op,npj->noj', output_inverse, half, preferred_e...]
    optimization_barrier x1 -> x0, local copies, waits for them, and re-layouts: 2.26 us -> none  [local(): sent, _ = lax.optimization_barrier((sent, ready))]
    dot_general x4 -> x2, matrix products: 9.56 us -> 8.31 us  [local(): jnp.einsum('nqf,sqmf->snm', conditioned.reshape(part, half_rows, query_wi...]
  transfers between devices with their start and end apart: 7 -> 6, of which waited for: 5 -> 3; matrix products, arithmetic and copies ran while one was open for 16% -> 17% of each run, Pallas kernels for 16% -> 31%
where the time goes in v3:
time: 184 us
  waiting for transfers between devices  64.2 us (35%)
  Pallas kernels  57.2 us (31%)
  matrix products  18.5 us (10%)
  local copies, waits for them, and re-layouts  15.3 us (8%)
  between operations  13.6 us (7%)
  starting transfers between devices  8.57 us (5%)
  other arithmetic  6.61 us (4%)
    pallas_call x1, Pallas kernels, sum_over_group(): pl.pallas_call(functools.partial(sum_kernel, rows, group), out_shape=jax....  50.1 us
    ppermute x2, waiting for transfers between devices, shifted(): return lax.ppermute(value, 'col', pairs)  43.6 us
    ppermute x2, waiting for transfers between devices, local(): results.append(kept + lax.ppermute(given, 'col', pairs).astype(jnp.float32))  20.6 us
    dot_general x2, matrix products, local(): jnp.einsum('nqf,sqmf->snm', conditioned.reshape(part, half_rows, query_wi...  8.31 us
    pallas_call x1, Pallas kernels, invert(): pl.pallas_call(functools.partial(invert_kernel, scale), out_shape=jax.Sha...  7.05 us
    convert_element_type x2, local copies, waits for them, and re-layouts, local(): conditioned = jnp.einsum('op,npj->noj', output_inverse, half, preferred_e...  5.11 us
    dot_general x1, matrix products, factor_terms(): jnp.einsum('noi,npi->op', block, block, preferred_element_type=jnp.float32)  4.42 us
    another operation x2, other arithmetic, local(): turns.append(jnp.stack(pieces, axis=1))  4.23 us
  transfers between devices with their start and end apart: 6, of which 3 were waited for; matrix products, arithmetic and copies ran while one was open for 17% of the time, Pallas kernels for 31%

profile of v3, /device:TPU:0, one launch (start us, length us, event | category | flops | bytes accessed | tf_op | source)
XLA Modules:
  0.0 184.0 jit_solution(9964114785854543322)
XLA Ops:
  6.5 1.9 %collective-permute-start.1 = (bf16[512,1024]{1,0:T(8,128)(2,1)}, bf16[512,1024]{1,0:T(8,128)(2,1)S(1)}, u32[]{:S(2)}, u32[]{:S(2)}) collective-permute-start(bf16[512,1024]{1,0:T(8,128)(2,1)} %param.3), channel_id=1, source_target_pairs={{0,0},{1,1},{2,16},{3,17},{4,4},{5,5},{6,20},{7,21},{8,8},{9,9},{1... | collective-permute-start | bytes 3145736 | tf_op jit(solution)/shard_map/ppermute | solution.py:156
  8.4 0.0 collective-permute-done.1
  8.4 1.0 copy-done.3
  9.4 0.0 all-gather.3.cloned.1.call-update
  9.5 3.2 %constant_dynamic-slice_fusion = (bf16[256,2048]{1,0:T(8,128)(2,1)S(1)}, bf16[256,1,2048]{2,0,1:T(8,128)(2,1)}, bf16[256,2048]{1,0:T(8,128)(2,1)S(1)}) fusion(bf16[512,2048]{1,0:T(8,128)(2,1)} %param.2, s32[]{:T(128)S(6)} %select_n.66, s32[]{:T(128)S(6)} %select_n.59, s32[]{:T(128)S(6)} %select_n.60), kind=kLoop, calls=%fused_computation.48 | loop fusion | bytes 6291468 | tf_op jit(solution)/shard_map/dynamic_slice | solution.py:128
  12.7 3.0 %collective-permute-start = (bf16[256,2048]{1,0:T(8,128)(2,1)S(1)}, bf16[256,2048]{1,0:T(8,128)(2,1)}, u32[]{:S(2)}, u32[]{:S(2)}) collective-permute-start(bf16[256,2048]{1,0:T(8,128)(2,1)S(1)} %get-tuple-element.7), channel_id=1, source_target_pairs={{0,1},{1,0},{2,3},{3,2},{4,5},{5,4},{6,7},{7,6},{8,9},{9,8},{10,11... | collective-permute-start | bytes 3145736 | tf_op jit(solution)/shard_map/ppermute | solution.py:125
  15.7 1.3 copy.27
  17.0 0.0 collective-permute-start.3
  17.0 0.5 copy.14
  17.6 43.6 %collective-permute-done = bf16[256,2048]{1,0:T(8,128)(2,1)} collective-permute-done((bf16[256,2048]{1,0:T(8,128)(2,1)S(1)}, bf16[256,2048]{1,0:T(8,128)(2,1)}, u32[]{:S(2)}, u32[]{:S(2)}) %collective-permute-start) | collective-permute-done | bytes 1048608 | tf_op jit(solution)/shard_map/ppermute | solution.py:125
  61.2 0.0 copy-done
  61.2 2.8 %pad_maximum_fusion = bf16[256,2,2048]{2,0,1:T(8,128)(2,1)} fusion(bf16[256,1,2048]{2,0,1:T(8,128)(2,1)} %bitcast.1, bf16[256,1,2048]{2,0,1:T(8,128)(2,1)S(1)} %copy-done), kind=kLoop, calls=%fused_computation.4 | loop fusion | flops 1048576 | bytes 4194304 | tf_op jit(solution)/shard_map/stack | solution.py:136
  64.0 2.8 %copy.6 = bf16[256,2,2048]{0,2,1:T(8,128)(2,1)S(1)} copy(bf16[256,2,2048]{2,0,1:T(8,128)(2,1)} %pad_maximum_fusion) | data formatting | bytes 4194304 | tf_op jit(solution)/shard_map/stack | solution.py:136
  66.8 4.4 %fusion.10 = f32[2,32,64]{2,1,0:T(8,128)S(1)} fusion(bf16[256,64,64]{0,2,1:T(8,128)(2,1)S(1)} %bitcast.97, bf16[2,32,64,256]{3,2,1,0:T(8,128)(2,1)S(1)} %bitcast.98), kind=kOutput, calls=%fused_computation.22 | convolution fusion | flops 134217728 | bytes 4210688 | tf_op jit(solution)/shard_map/noi,npi->op/dot_general | solution.py:20
  71.3 0.1 concatenate.17
  71.4 0.1 concatenate.18
  71.5 0.1 constant_dynamic-slice_fusion.2
  71.6 0.1 maximum_bitcast_fusion
  71.6 0.7 convolution_bitcast_fusion.2
  72.3 0.6 pad_maximum_fusion.3.x_ref
  73.0 50.1 %shard_map.28.x_ref = f32[2,64,64]{2,1,0:T(8,128)} custom-call(f32[2,64,64]{2,1,0:T(8,128)} %pad_maximum_fusion.3.x_ref), custom_call_target="tpu_custom_call" | custom-call | tf_op jit(solution)/shard_map/pallas_call | solution.py:61
  123.1 7.0 %shard_map.29 = bf16[2,64,64]{2,1,0:T(8,128)(2,1)} custom-call(f32[2,64,64]{2,1,0:T(8,128)} %shard_map.28.x_ref), custom_call_target="tpu_custom_call" | custom-call | tf_op jit(solution)/shard_map/pallas_call | solution.py:100
  130.1 0.7 slice.29
  130.9 0.1 copy.9
  131.0 0.1 copy.10
  131.1 0.1 copy.11
  131.2 0.0 collective-permute-done.3
  131.2 0.0 copy-start.4
  131.2 1.4 pad_maximum_fusion.1
  132.6 0.8 fusion.23
  133.4 1.7 convert_bitcast_fusion
  135.1 2.5 %copy.16 = bf16[256,64,64]{0,2,1:T(8,128)(2,1)} copy(bf16[256,64,64]{0,1,2:T(8,128)(2,1)S(1)} %convert_bitcast_fusion) | data formatting | bytes 4194304 | tf_op jit(solution)/shard_map/convert_element_type | solution.py:173
  137.6 0.8 fusion.24
  138.4 1.9 %convert_bitcast_fusion.1 = bf16[256,64,64]{0,1,2:T(8,128)(2,1)S(1)} fusion(bf16[256,64,64]{0,2,1:T(8,128)(2,1)S(1)} %fusion.24, bf16[64,32]{1,0:T(8,128)(2,1)S(1)} %copy.11, bf16[64,32]{1,0:T(8,128)(2,1)S(1)} %copy.10), kind=kOutput, calls=%fused_computation.11 | convolution fusion | flops 135282688 | bytes 4202496 | tf_op jit(solution)/shard_map/op,npj->noj/dot_general | solution.py:171
  140.3 2.6 %copy.12 = bf16[256,64,64]{0,2,1:T(8,128)(2,1)} copy(bf16[256,64,64]{0,1,2:T(8,128)(2,1)S(1)} %convert_bitcast_fusion.1) | data formatting | bytes 4194304 | tf_op jit(solution)/shard_map/convert_element_type | solution.py:173
  142.9 5.9 %fusion.9 = f32[2,256,512]{2,1,0:T(8,128)S(1)} fusion(bf16[256,4,1024,1]{0,2,1,3:T(8,128)(2,1)S(1)} %bitcast.103, bf16[2,4,512,1024]{3,2,1,0:T(8,128)(2,1)} %bitcast.108), kind=kOutput, calls=%fused_computation.17 | convolution fusion | flops 2147745792 | bytes 11534336 | tf_op jit(solution)/shard_map/nqf,sqmf->snm/dot_general | solution.py:175
  148.8 0.1 fusion.22
  148.9 3.3 %collective-permute-start.4 = (bf16[256,512]{1,0:T(8,128)(2,1)S(1)}, bf16[256,512]{1,0:T(8,128)(2,1)S(1)}, u32[]{:S(2)}, u32[]{:S(2)}) collective-permute-start(bf16[256,512]{1,0:T(8,128)(2,1)S(1)} %fusion.22), channel_id=1, source_target_pairs={{0,2},{1,3},{2,0},{3,1},{4,6},{5,7},{6,4},{7,5},{8,10},{9,11},{10,... | collective-permute-start | bytes 786440 | tf_op jit(solution)/shard_map/ppermute | solution.py:184
  152.1 0.0 copy-done.2
  152.1 2.4 %fusion.7 = f32[2,256,512]{2,1,0:T(8,128)S(1)} fusion(bf16[256,4,1024,1]{0,2,1,3:T(8,128)(2,1)S(1)} %bitcast.104, bf16[2,4,512,1024]{3,2,1,0:T(8,128)(2,1)S(1)} %bitcast.109), kind=kOutput, calls=%fused_computation.15 | convolution fusion | flops 2147745792 | bytes 11534336 | tf_op jit(solution)/shard_map/nqf,sqmf->snm/dot_general | solution.py:175
  154.5 0.1 fusion.21
  154.6 0.4 collective-permute-start.2
  155.0 15.1 %collective-permute-done.4 = bf16[256,512]{1,0:T(8,128)(2,1)S(1)} collective-permute-done((bf16[256,512]{1,0:T(8,128)(2,1)S(1)}, bf16[256,512]{1,0:T(8,128)(2,1)S(1)}, u32[]{:S(2)}, u32[]{:S(2)}) %collective-permute-start.4) | collective-permute-done | bytes 262176 | tf_op jit(solution)/shard_map/ppermute | solution.py:184
  170.1 0.1 fusion.19
  170.2 5.5 %collective-permute-done.2 = bf16[256,512]{1,0:T(8,128)(2,1)S(1)} collective-permute-done((bf16[256,512]{1,0:T(8,128)(2,1)S(1)}, bf16[256,512]{1,0:T(8,128)(2,1)S(1)}, u32[]{:S(2)}, u32[]{:S(2)}) %collective-permute-start.2) | collective-permute-done | bytes 262176 | tf_op jit(solution)/shard_map/ppermute | solution.py:184
  175.7 0.1 fusion.20
  175.8 0.3 fusion.18
  176.1 1.0 pad_maximum_fusion.2
  (14 shorter events, 0.1 us)
Async XLA Ops:
  6.5 136.3 %all-gather.3.cloned.1.call-start = ((), (), s32[]{:S(2)}) async-start(), calls=%async_computation | async-start | bytes 9437184 | tf_op jit(solution)/shard_map/all_gather | solution.py:159
  6.5 1.9 %collective-permute-start.1 = (bf16[512,1024]{1,0:T(8,128)(2,1)}, bf16[512,1024]{1,0:T(8,128)(2,1)S(1)}, u32[]{:S(2)}, u32[]{:S(2)}) collective-permute-start(bf16[512,1024]{1,0:T(8,128)(2,1)} %param.3), channel_id=1, source_target_pairs={{0,0},{1,1},{2,16},{3,17},{4,4},{5,5},{6,20},{7,21},{8,8},{9,9},{1... | collective-permute-start | bytes 3145736 | tf_op jit(solution)/shard_map/ppermute | solution.py:156
  8.4 1.0 copy-start.3
  12.7 48.5 %collective-permute-start = (bf16[256,2048]{1,0:T(8,128)(2,1)S(1)}, bf16[256,2048]{1,0:T(8,128)(2,1)}, u32[]{:S(2)}, u32[]{:S(2)}) collective-permute-start(bf16[256,2048]{1,0:T(8,128)(2,1)S(1)} %get-tuple-element.7), channel_id=1, source_target_pairs={{0,1},{1,0},{2,3},{3,2},{4,5},{5,4},{6,7},{7,6},{8,9},{9,8},{10,11... | collective-permute-start | bytes 3145736 | tf_op jit(solution)/shard_map/ppermute | solution.py:125
  17.0 44.1 %copy-start = (bf16[256,1,2048]{2,0,1:T(8,128)(2,1)S(1)}, bf16[256,1,2048]{2,0,1:T(8,128)(2,1)}, u32[]{:S(2)}) copy-start(bf16[256,1,2048]{2,0,1:T(8,128)(2,1)} %get-tuple-element.6) | copy-start | bytes 3145732
  17.0 114.2 %collective-permute-start.3 = (bf16[256,2048]{0,1:T(8,128)(2,1)}, bf16[256,2048]{0,1:T(8,128)(2,1)}, u32[]{:S(2)}, u32[]{:S(2)}) collective-permute-start(bf16[256,2048]{0,1:T(8,128)(2,1)} %copy.27), channel_id=1, source_target_pairs={{0,1},{1,0},{2,3},{3,2},{4,5},{5,4},{6,7},{7,6},{8,9},{9,8},{10,11... | collective-permute-start | bytes 3145736 | tf_op jit(solution)/shard_map/ppermute | solution.py:125
  131.2 1.4 copy-start.4
  140.3 2.6 %copy-start.1 = (bf16[256,64,64]{0,2,1:T(8,128)(2,1)S(1)}, bf16[256,64,64]{0,2,1:T(8,128)(2,1)}, u32[]{:S(2)}) copy-start(bf16[256,64,64]{0,2,1:T(8,128)(2,1)} %copy.16) | copy-start | bytes 6291460
  142.9 9.3 %copy-start.2 = (bf16[256,64,64]{0,2,1:T(8,128)(2,1)S(1)}, bf16[256,64,64]{0,2,1:T(8,128)(2,1)}, u32[]{:S(2)}) copy-start(bf16[256,64,64]{0,2,1:T(8,128)(2,1)} %copy.12) | copy-start | bytes 6291460
  142.9 9.3 %copy-start.5 = (bf16[4096,1024]{1,0:T(8,128)(2,1)S(1)}, bf16[4096,1024]{1,0:T(8,128)(2,1)}, u32[]{:S(2)}) copy-start(bf16[4096,1024]{1,0:T(8,128)(2,1)} %all-gather.3.cloned.1.call-done) | copy-start | bytes 25165828
  148.9 21.2 %collective-permute-start.4 = (bf16[256,512]{1,0:T(8,128)(2,1)S(1)}, bf16[256,512]{1,0:T(8,128)(2,1)S(1)}, u32[]{:S(2)}, u32[]{:S(2)}) collective-permute-start(bf16[256,512]{1,0:T(8,128)(2,1)S(1)} %fusion.22), channel_id=1, source_target_pairs={{0,2},{1,3},{2,0},{3,1},{4,6},{5,7},{6,4},{7,5},{8,10},{9,11},{10,... | collective-permute-start | bytes 786440 | tf_op jit(solution)/shard_map/ppermute | solution.py:184
  154.6 21.1 %collective-permute-start.2 = (bf16[256,512]{1,0:T(8,128)(2,1)S(1)}, bf16[256,512]{1,0:T(8,128)(2,1)S(1)}, u32[]{:S(2)}, u32[]{:S(2)}) collective-permute-start(bf16[256,512]{1,0:T(8,128)(2,1)S(1)} %fusion.21), channel_id=1, source_target_pairs={{0,2},{1,3},{2,0},{3,1},{4,6},{5,7},{6,4},{7,5},{8,10},{9,11},{10,... | collective-permute-start | bytes 786440 | tf_op jit(solution)/shard_map/ppermute | solution.py:184
Sparse Core Ops, SparseCore 0:
  9.6 121.7 all-gather.2
